TPU v7x, 1024 devices: a whole 4x4x32 slice. The times are simulated.
1024 devices in a mesh: replica: 4 (over y_lo, core), fsdp: 256 (over z, y_hi, x).
Axes of the slice: x: 4, y: 4 (y_hi: 2, y_lo: 2; y = y_hi * 2 + y_lo), z: 32, core: 2. Of those that a mesh axis runs over, the one named last changes fastest.
Arguments:
- inner_stack: bfloat16 [4, 4, 4096, 512], P('replica', None, 'fsdp'), may hold values from -6 to 6
- outer_stack: float32 [4, 4096, 512], P(None, 'fsdp'), may hold values from -6 to 6
- outer_moment: float32 [4, 4096, 512], P(None, 'fsdp'), may hold values from -4 to 4
- layer_ids: int32 [4], replicated, may hold values from 0 to 3, each once
- step_count: int32 [1], replicated, may hold values from 0 to 63
- activations: bfloat16 [262144, 4096], P(('replica', 'fsdp')), may hold values from -24 to 24
- cotangent: bfloat16 [262144, 512], P(('replica', 'fsdp')), may hold values from -0.0625 to 0.0625
- key_weight: bfloat16 [4, 4096, 512], P('replica', 'fsdp'), may hold values from -6 to 6
- first_moment: float32 [4, 4096, 512], P('replica', 'fsdp'), may hold values from -4 to 4
- second_moment: float32 [4, 4096, 512], P('replica', 'fsdp'), may hold values from 0.05 to 2
Outputs:
- inner_out: bfloat16 [4, 4, 4096, 512], P('replica', None, 'fsdp')
- outer_out: float32 [4, 4096, 512], P(None, 'fsdp')
- moment_out: float32 [4, 4096, 512], P(None, 'fsdp')
- key_out: bfloat16 [4, 4096, 512], P('replica', 'fsdp')
- first_out: float32 [4, 4096, 512], P('replica', 'fsdp')
- second_out: float32 [4, 4096, 512], P('replica', 'fsdp')
Inputs may be any that keep to these rules, and one draw needn't show every extreme that they name: `layer_ids`: each layer index appears once.
All inputs are finite; a program needn't handle non-finite values.
Results may differ from a plain program's by a relative error of at most 0.012.
Values may be sent and summed in bfloat16 or wider, within the bound.
A program may use at most 32 MiB of HBM per device.

v0:
```python
import jax
import jax.numpy as jnp
from jax import lax
from jax.sharding import PartitionSpec as P

BLOCK = 128
FRAG_LAYERS = 1
FRAGS = 4


BETA_FIRST = 0.9
BETA_SECOND = 0.95
INNER_RATE = 0.05
DECAY_RATE = 0.1
ADAM_EPSILON = 1e-08
OUTER_RATE = 0.7
OUTER_MOMENTUM = 0.9
CODE_LIMIT = 448.0
SCALE_EPSILON = 1e-06


def fragment_ids(layer_ids, step_count):
    fragment = step_count[0] % FRAGS
    return lax.dynamic_slice(layer_ids, (fragment * FRAG_LAYERS,), (FRAG_LAYERS,))


def encode_blocks(deltas):
    shaped = deltas.reshape(deltas.shape[:-1] + (deltas.shape[-1] // BLOCK, BLOCK))
    scales = jnp.max(jnp.abs(shaped), axis=-1) / CODE_LIMIT + SCALE_EPSILON
    encoded = (shaped / scales[..., None]).astype(jnp.bfloat16)
    return (encoded, scales)


def decode_blocks(encoded, scales):
    decoded = encoded.astype(jnp.float32) * scales[..., None]
    return decoded.reshape(decoded.shape[:-2] + (decoded.shape[-2] * decoded.shape[-1],))


def outer_update(outer_frag, moment_frag, summed, groups):
    average = summed / groups
    moment_new = OUTER_MOMENTUM * moment_frag + average
    outer_new = outer_frag - OUTER_RATE * (OUTER_MOMENTUM * moment_new + average)
    return (outer_new, moment_new)


def adam_update(weight, first, second, gradient, step_count):
    counter = (step_count[0] + 1).astype(jnp.float32)
    first_new = BETA_FIRST * first + (1.0 - BETA_FIRST) * gradient
    second_new = BETA_SECOND * second + (1.0 - BETA_SECOND) * gradient * gradient
    first_hat = first_new / (1.0 - jnp.power(jnp.float32(BETA_FIRST), counter))
    second_hat = second_new / (1.0 - jnp.power(jnp.float32(BETA_SECOND), counter))
    widened = weight.astype(jnp.float32)
    moved = widened - INNER_RATE * (
        first_hat / (jnp.sqrt(second_hat) + ADAM_EPSILON) + DECAY_RATE * widened
    )
    return (moved.astype(jnp.bfloat16), first_new, second_new)


def replica_total(encoded, scales):
    return lax.psum(decode_blocks(encoded, scales)[0].astype(jnp.bfloat16), "replica").astype(
        jnp.float32
    )


def group_gradient(activations, cotangent):
    return lax.psum_scatter(
        lax.dot_general(
            activations, cotangent, (((0,), (0,)), ((), ())), preferred_element_type=jnp.float32
        ),
        "fsdp",
        scatter_dimension=0,
        tiled=True,
    )[None]


def on_device(
    inner_stack,
    outer_stack,
    outer_moment,
    layer_ids,
    step_count,
    activations,
    cotangent,
    key_weight,
    first_moment,
    second_moment,
):
    frag_ids = fragment_ids(layer_ids, step_count)
    outer_frag = jnp.take(outer_stack, frag_ids, axis=0)
    moment_frag = jnp.take(outer_moment, frag_ids, axis=0)
    inner_frag = jnp.take(inner_stack, frag_ids, axis=1).astype(jnp.float32)
    deltas = outer_frag[None] - inner_frag
    groups = lax.axis_size("replica")
    encoded, scales = encode_blocks(deltas)
    summed = replica_total(encoded, scales)
    gradient = group_gradient(activations, cotangent)
    outer_new, moment_new = outer_update(outer_frag, moment_frag, summed, groups)
    outer_out = outer_stack.at[frag_ids].set(outer_new)
    moment_out = outer_moment.at[frag_ids].set(moment_new)
    rounded = outer_new.astype(jnp.bfloat16)[None]
    inner_out = inner_stack.at[:, frag_ids].set(rounded)
    key_out, first_out, second_out = adam_update(
        key_weight, first_moment, second_moment, gradient, step_count
    )
    return (inner_out, outer_out, moment_out, key_out, first_out, second_out)


def solution(mesh):
    return jax.shard_map(
        on_device,
        mesh=mesh,
        in_specs=(
            P("replica", None, "fsdp", None),
            P(None, "fsdp", None),
            P(None, "fsdp", None),
            P(),
            P(),
            P(("replica", "fsdp"), None),
            P(("replica", "fsdp"), None),
            P("replica", "fsdp", None),
            P("replica", "fsdp", None),
            P("replica", "fsdp", None),
        ),
        out_specs=(
            P("replica", None, "fsdp", None),
            P(None, "fsdp", None),
            P(None, "fsdp", None),
            P("replica", "fsdp", None),
            P("replica", "fsdp", None),
            P("replica", "fsdp", None),
        ),
        check_vma=False,
    )
```

profile of v0, /device:TPU:6, one launch (start us, length us, event | category | flops | bytes accessed | tf_op | source)
XLA Modules:
  0.0 1467.0 jit_solution(13007150737788503354)
XLA Ops:
  7.2 0.0 copy-start
  7.2 0.0 reduce-scatter.2.cloned.1.call-start
  7.2 1.0 copy.23
  8.2 0.9 copy.24
  9.1 0.9 copy.25
  10.0 0.0 copy-done
  10.0 5.5 fusion.10
  15.5 0.0 copy-start.9
  15.5 0.0 copy-start.8
  15.5 0.0 copy-start.7
  15.5 0.0 copy-start.4
  15.5 0.0 copy-start.5
  15.5 0.0 copy-start.6
  15.5 0.0 reduce-scatter.2.cloned.1.call-update
  16.3 0.0 copy-done.9
  16.3 0.6 dynamic_slice.3
  19.0 0.1 abs_reduce_fusion
  19.1 0.1 div.41
  19.2 11.3 psum.7
  30.5 0.0 copy-done.8
  30.5 0.7 and_reduce_fusion
  31.2 0.0 copy-done.7
  31.2 0.7 and_reduce_fusion.1
  31.9 0.7 fusion.8
  32.6 0.0 copy-start.3
  32.6 0.7 select_dynamic-update-slice_fusion
  33.3 0.0 copy-start.1
  33.3 0.0 copy-start.2
  33.3 1425.4 %reduce-scatter.2.cloned.1.call-done = f32[16,512]{1,0:T(8,128)} async-done(((f32[4096,512]{1,0:T(8,128)}), f32[16,512]{1,0:T(8,128)}) %reduce-scatter.2.cloned.1.call-update) | async-done | bytes 32784 | tf_op jit(solution)/shard_map/reduce_scatter | solution.py:66
  1458.8 0.0 copy-done.4
  1458.8 0.0 copy-done.5
  1458.8 0.0 copy-done.6
  1458.8 1.4 fusion.2
  1460.2 0.0 copy-done.3
  1460.2 0.0 copy-done.1
  1460.2 0.0 copy-done.2
  (7 shorter events, 0.1 us)
Async XLA Ops:
  7.2 2.9 copy-start
  7.2 1451.6 %reduce-scatter.2.cloned.1.call-start = ((), (), s32[]{:S(2)}) async-start(), calls=%async_computation.1 | async-start | bytes 8421376 | tf_op jit(solution)/shard_map/reduce_scatter | solution.py:66
  15.5 0.9 copy-start.9
  15.5 15.0 %copy-start.8 = (s32[3]{0:T(128)S(1)}, s32[3]{0:T(128)}, u32[]{:S(2)}) copy-start(s32[3]{0:T(128)} %constant.128.clone.1) | copy-start | bytes 40
  15.5 15.7 %copy-start.7 = (s32[4]{0:T(128)S(1)}, s32[4]{0:T(128)}, u32[]{:S(2)}) copy-start(s32[4]{0:T(128)} %constant.117.clone.1) | copy-start | bytes 52
  15.5 1443.3 %copy-start.4 = (f32[1,16,512]{2,1,0:T(8,128)S(1)}, f32[1,16,512]{2,1,0:T(8,128)}, u32[]{:S(2)}) copy-start(f32[1,16,512]{2,1,0:T(8,128)} %param.27) | copy-start | bytes 98308
  15.5 1443.3 %copy-start.5 = (f32[1,16,512]{2,1,0:T(8,128)S(1)}, f32[1,16,512]{2,1,0:T(8,128)}, u32[]{:S(2)}) copy-start(f32[1,16,512]{2,1,0:T(8,128)} %param.26) | copy-start | bytes 98308
  15.5 1443.3 %copy-start.6 = (bf16[1,16,512]{2,1,0:T(8,128)(2,1)S(1)}, bf16[1,16,512]{2,1,0:T(8,128)(2,1)}, u32[]{:S(2)}) copy-start(bf16[1,16,512]{2,1,0:T(8,128)(2,1)} %param.25) | copy-start | bytes 49156
  32.6 1427.6 %copy-start.3 = (bf16[1,4,16,512]{3,2,1,0:T(8,128)(2,1)}, bf16[1,4,16,512]{3,2,1,0:T(8,128)(2,1)S(1)}, u32[]{:S(2)}) copy-start(bf16[1,4,16,512]{3,2,1,0:T(8,128)(2,1)S(1)} %fusion.8) | copy-start | bytes 196612
  33.3 1426.9 %copy-start.1 = (f32[4,16,512]{2,1,0:T(8,128)}, f32[4,16,512]{2,1,0:T(8,128)S(1)}, u32[]{:S(2)}) copy-start(f32[4,16,512]{2,1,0:T(8,128)S(1)} %get-tuple-element.69) | copy-start | bytes 393220
  33.3 1426.9 %copy-start.2 = (f32[4,16,512]{2,1,0:T(8,128)}, f32[4,16,512]{2,1,0:T(8,128)S(1)}, u32[]{:S(2)}) copy-start(f32[4,16,512]{2,1,0:T(8,128)S(1)} %get-tuple-element.68) | copy-start | bytes 393220
Sparse Core Ops, SparseCore 0:
  15.7 1443.0 reduce-scatter.1
where the time goes:
time: 1480 us; the launch traced here: 1470 us
  waiting for transfers between devices  1430 us (97%)
  between operations  16.9 us (1%)
    reduce_scatter x1, waiting for transfers between devices, group_gradient(): lax.psum_scatter(lax.dot_general(activations, cotangent, (((0,), (0,)), (...  1430 us
  transfers between devices with their start and end apart: 1, of which 1 were waited for; matrix products, arithmetic and copies ran while one was open for 0% of the time, Pallas kernels for 0%

commit v1 on v0

v1 whole, which is shorter than its diff:
```python
import jax
import jax.numpy as jnp
from jax import lax
from jax.experimental import pallas as pl
from jax.experimental.pallas import tpu as pltpu
from jax.sharding import PartitionSpec as P

BLOCK = 128
FRAG_LAYERS = 1
FRAGS = 4

BETA_FIRST = 0.9
BETA_SECOND = 0.95
INNER_RATE = 0.05
DECAY_RATE = 0.1
ADAM_EPSILON = 1e-08
OUTER_RATE = 0.7
OUTER_MOMENTUM = 0.9
CODE_LIMIT = 448.0
SCALE_EPSILON = 1e-06

ROWS = 16
COLS = 512
PLANES = 8
BLOCKS = 32
MESH = pl.DeviceIdType.MESH

CHUNKS = (
    (4, "aby"),
    (3, "bay"),
    (5, "yab"),
    (2, "aby"),
    (6, "bay"),
    (1, "yba"),
    (7, "aby"),
    (0, "bay"),
)
LAGS = (2, 3, 4, 5)


def outer_update(outer_frag, moment_frag, summed, groups):
    average = summed / groups
    moment_new = OUTER_MOMENTUM * moment_frag + average
    outer_new = outer_frag - OUTER_RATE * (OUTER_MOMENTUM * moment_new + average)
    return (outer_new, moment_new)


def adam_update(weight, first, second, gradient, step_count):
    counter = (step_count[0] + 1).astype(jnp.float32)
    first_new = BETA_FIRST * first + (1.0 - BETA_FIRST) * gradient
    second_new = BETA_SECOND * second + (1.0 - BETA_SECOND) * gradient * gradient
    first_hat = first_new / (1.0 - jnp.power(jnp.float32(BETA_FIRST), counter))
    second_hat = second_new / (1.0 - jnp.power(jnp.float32(BETA_SECOND), counter))
    widened = weight.astype(jnp.float32)
    moved = widened - INNER_RATE * (
        first_hat / (jnp.sqrt(second_hat) + ADAM_EPSILON) + DECAY_RATE * widened
    )
    return (moved.astype(jnp.bfloat16), first_new, second_new)


def exchange(
    step_ref, ids_ref, inner_ref, outer_ref, act_ref, cot_ref,
    grad_ref, sum_ref,
    work, got0, got1, got2, got3, got4, terms,
    send, recv, term_send, term_recv,
):
    rep = lax.axis_index("replica")
    me = lax.axis_index("fsdp")
    x = lax.rem(me, 4)
    y = lax.rem(me // 4, 2)
    z = me // 8
    low = lax.rem(z, 4)
    high = z // 4
    a = lax.rem((x + 1) // 2, 2)
    b = x // 2

    def at(x_to, y_to, low_to, high_to):
        return (rep, ((high_to * 4 + low_to) * 2 + y_to) * 4 + x_to)

    near = {
        "a": at(x + 1 - 2 * lax.rem(x, 2), y, low, high),
        "b": at(3 - x, y, low, high),
        "y": at(x, 1 - y, low, high),
    }
    lows = [at(x, y, lax.rem(low + i, 4), high) for i in range(1, 4)]
    highs = {d: at(x, y, low, lax.rem(high + d, PLANES)) for d in range(1, PLANES)}
    reps = [(lax.rem(rep + i, 4), me) for i in range(1, 4)]

    barrier = pltpu.get_barrier_semaphore()
    peers = [*near.values(), *lows, *highs.values(), *reps]
    for peer in peers:
        pl.semaphore_signal(barrier, inc=1, device_id=peer, device_id_type=MESH)

    def remote(src, dst, sems, k, peer):
        return pltpu.make_async_remote_copy(
            src_ref=src, dst_ref=dst, send_sem=sems[0].at[k], recv_sem=sems[1].at[k],
            device_id=peer, device_id_type=MESH,
        )

    frag = ids_ref[lax.rem(step_ref[0], FRAGS)]
    deltas = outer_ref[frag] - inner_ref[0, frag].astype(jnp.float32)
    for k in range(COLS // BLOCK):
        part = deltas[:, k * BLOCK : (k + 1) * BLOCK]
        scale = jnp.max(jnp.abs(part), axis=-1, keepdims=True) / CODE_LIMIT + SCALE_EPSILON
        coded = (part / scale).astype(jnp.bfloat16).astype(jnp.float32)
        terms[rep, :, k * BLOCK : (k + 1) * BLOCK] = (coded * scale).astype(jnp.bfloat16)

    def multiply(c):
        ahead, order = CHUNKS[c]
        first = pl.multiple_of(lax.rem(high + ahead, PLANES) * 512, 512)
        part = lax.dot_general(
            act_ref[:, pl.ds(first, 512)], cot_ref[...], (((0,), (0,)), ((), ())),
            preferred_element_type=jnp.float32,
        ).astype(jnp.bfloat16)
        for n in range(BLOCKS):
            low_to, y_to, x_to = n // 8, (n // 4) % 2, n % 4
            off = {
                "a": lax.rem(a + ((x_to + 1) // 2) % 2, 2),
                "b": lax.rem(b + x_to // 2, 2),
                "y": lax.rem(y + y_to, 2),
            }
            place = lax.rem(low_to - low + 4, 4)
            for weight, axis in zip((16, 8, 4), order):
                place = place + off[axis] * weight
            work[c, place] = part[n * ROWS : (n + 1) * ROWS]

    def sends(c, stage):
        ahead, order = CHUNKS[c]
        sems = (send.at[c], recv.at[c])
        if stage < 3:
            got, n = ((got0, 16), (got1, 8), (got2, 4))[stage]
            return [remote(work.at[c, pl.ds(n, n)], got.at[c], sems, stage, near[order[stage]])]
        if stage == 3:
            return [
                remote(work.at[c, i], got3.at[c, i - 1], sems, 2 + i, lows[i - 1])
                for i in range(1, 4)
            ]
        return [remote(work.at[c, 0], got4.at[ahead - 1], sems, 6, highs[ahead])] if ahead else []

    def add(c, got, n):
        def some(i, carry):
            rows = pl.ds(i * 4, 4)
            total = work[c, rows].astype(jnp.float32) + got[c, rows].astype(jnp.float32)
            work[c, rows] = total.astype(jnp.bfloat16)
            return carry

        lax.fori_loop(0, n // 4, some, 0)

    def advance(c, stage):
        for copy in sends(c, stage):
            copy.wait_recv()
        if stage < 3:
            add(c, (got0, got1, got2)[stage], (16, 8, 4)[stage])
        else:
            total = work[c, 0].astype(jnp.float32)
            for i in range(3):
                total = total + got3[c, i].astype(jnp.float32)
            if CHUNKS[c][0]:
                work[c, 0] = total.astype(jnp.bfloat16)
            else:
                grad_ref[...] = total
        for copy in sends(c, stage + 1):
            copy.start()

    count = len(CHUNKS)
    multiply(0)
    pl.semaphore_wait(barrier, len(peers))
    swaps = [
        remote(terms.at[rep], terms.at[rep], (term_send, term_recv), i, reps[i]) for i in range(3)
    ]
    for t in range(count + LAGS[-1]):
        if t < count:
            if t:
                multiply(t)
            for copy in sends(t, 0):
                copy.start()
        if t == 0:
            for copy in swaps:
                copy.start()
        for stage, lag in enumerate(LAGS):
            if 0 <= t - lag < count:
                advance(t - lag, stage)

    for copy in swaps:
        copy.wait()
    total = terms[0].astype(jnp.float32)
    for i in range(1, 4):
        total = total + terms[i].astype(jnp.float32)
    sum_ref[...] = total

    total = grad_ref[...]
    for c in range(count):
        for copy in sends(c, 4):
            copy.wait_recv()
            total = total + got4[CHUNKS[c][0] - 1].astype(jnp.float32)
    grad_ref[...] = total
    for c in range(count):
        for stage in range(5):
            for copy in sends(c, stage):
                copy.wait_send()


def exchanged(step_count, layer_ids, inner_stack, outer_stack, activations, cotangent):
    vmem = pl.BlockSpec(memory_space=pltpu.VMEM)
    smem = pl.BlockSpec(memory_space=pltpu.SMEM)
    n = len(CHUNKS)
    block = (ROWS, COLS)
    tokens, features = activations.shape
    return pl.pallas_call(
        exchange,
        name="exchange",
        out_shape=(jax.ShapeDtypeStruct(block, jnp.float32),) * 2,
        in_specs=[smem, smem, vmem, vmem, vmem, vmem],
        out_specs=(vmem, vmem),
        scratch_shapes=[
            pltpu.VMEM((n, BLOCKS) + block, jnp.bfloat16),
            pltpu.VMEM((n, 16) + block, jnp.bfloat16),
            pltpu.VMEM((n, 8) + block, jnp.bfloat16),
            pltpu.VMEM((n, 4) + block, jnp.bfloat16),
            pltpu.VMEM((n, 3) + block, jnp.bfloat16),
            pltpu.VMEM((PLANES - 1,) + block, jnp.bfloat16),
            pltpu.VMEM((4,) + block, jnp.bfloat16),
            pltpu.SemaphoreType.DMA((n, 7)),
            pltpu.SemaphoreType.DMA((n, 7)),
            pltpu.SemaphoreType.DMA((3,)),
            pltpu.SemaphoreType.DMA((3,)),
        ],
        compiler_params=pltpu.CompilerParams(
            collective_id=0, has_side_effects=True, vmem_limit_bytes=40 * 2**20
        ),
        cost_estimate=pl.CostEstimate(
            flops=2 * tokens * features * COLS, bytes_accessed=2 * tokens * features, transcendentals=0
        ),
    )(step_count, layer_ids, inner_stack, outer_stack, activations, cotangent)


def on_device(
    inner_stack,
    outer_stack,
    outer_moment,
    layer_ids,
    step_count,
    activations,
    cotangent,
    key_weight,
    first_moment,
    second_moment,
):
    gradient, summed = exchanged(
        step_count, layer_ids, inner_stack, outer_stack, activations, cotangent
    )
    fragment = step_count[0] % FRAGS
    frag_ids = lax.dynamic_slice(layer_ids, (fragment * FRAG_LAYERS,), (FRAG_LAYERS,))
    outer_frag = jnp.take(outer_stack, frag_ids, axis=0)
    moment_frag = jnp.take(outer_moment, frag_ids, axis=0)
    outer_new, moment_new = outer_update(outer_frag, moment_frag, summed[None], 4)
    outer_out = outer_stack.at[frag_ids].set(outer_new)
    moment_out = outer_moment.at[frag_ids].set(moment_new)
    rounded = outer_new.astype(jnp.bfloat16)[None]
    inner_out = inner_stack.at[:, frag_ids].set(rounded)
    key_out, first_out, second_out = adam_update(
        key_weight, first_moment, second_moment, gradient[None], step_count
    )
    return (inner_out, outer_out, moment_out, key_out, first_out, second_out)


def solution(mesh):
    return jax.shard_map(
        on_device,
        mesh=mesh,
        in_specs=(
            P("replica", None, "fsdp", None),
            P(None, "fsdp", None),
            P(None, "fsdp", None),
            P(),
            P(),
            P(("replica", "fsdp"), None),
            P(("replica", "fsdp"), None),
            P("replica", "fsdp", None),
            P("replica", "fsdp", None),
            P("replica", "fsdp", None),
        ),
        out_specs=(
            P("replica", None, "fsdp", None),
            P(None, "fsdp", None),
            P(None, "fsdp", None),
            P("replica", "fsdp", None),
            P("replica", "fsdp", None),
            P("replica", "fsdp", None),
        ),
        check_vma=False,
    )
```

time: 1480 us -> 98.6 us (0.07)
  the two profiles are of different devices: /device:TPU:6 before, /device:TPU:2 now
where the time goes in v1:
time: 98.6 us; the launch traced here: 98.1 us
  Pallas kernels  82.3 us (83%)
  local copies, waits for them, and re-layouts  7.81 us (8%)
  other arithmetic  4.63 us (5%)
  between operations  3.4 us (3%)
    pallas_call x1, Pallas kernels, exchanged(): pl.pallas_call(exchange, name='exchange', out_shape=(jax.ShapeDtypeStruct...  82.3 us
    unnamed x21, local copies, waits for them, and re-layouts  6.57 us
    another operation x2, other arithmetic  2.74 us

profile of v1, /device:TPU:2, one launch (start us, length us, event | category | flops | bytes accessed | tf_op | source)
XLA Modules:
  0.0 98.1 jit_solution(8793546664544832055)
XLA Ops:
  0.6 0.9 copy.25
  1.5 0.9 copy.24.outer_ref
  2.4 0.0 copy-start.8
  2.4 0.9 copy.23.inner_ref
  3.3 0.0 copy-start.6
  3.3 0.0 copy-start.7
  4.1 1.2 %dynamic_slice.3 = s32[1]{0:T(128)} dynamic-slice(s32[4]{0:T(128)} %ids_ref.1, s32[]{:T(128)S(6)} %select_n.31), dynamic_slice_sizes={1} | dynamic-slice | bytes 12 | tf_op jit(solution)/shard_map/dynamic_slice | solution.py:253
  7.3 1.4 %and_reduce_fusion = pred[]{:T(512)} fusion(s32[3]{0:T(128)} %constant.106.clone.1, s32[1]{0:T(128)} %constant.97.clone.1, s32[1]{0:T(128)} %select_n.32), kind=kLoop, calls=%fused_computation.18 | loop fusion | flops 17 | bytes 21 | tf_op jit(solution)/shard_map/reduce.4
  8.6 1.4 %and_reduce_fusion.1 = pred[]{:T(512)} fusion(s32[4]{0:T(128)} %constant.101.clone.1, s32[1]{0:T(128)} %constant.97.clone.1, s32[1]{0:T(128)} %select_n.32), kind=kLoop, calls=%fused_computation.19 | loop fusion | flops 27 | bytes 25 | tf_op jit(solution)/shard_map/reduce.3
  10.0 0.0 copy-start.2
  10.0 1.6 %copy-done.2 = bf16[256,4096]{1,0:T(8,128)(2,1)S(1)} copy-done((bf16[256,4096]{1,0:T(8,128)(2,1)S(1)}, bf16[256,4096]{1,0:T(8,128)(2,1)}, u32[]{:S(2)}) %copy-start.2) | copy-done | bytes 2097176
  11.6 0.0 copy-start.3
  11.6 0.9 copy-done.3
  12.5 0.0 copy-start.4
  12.5 0.7 copy-done.4
  13.2 82.3 %exchange.1 = (f32[16,512]{1,0:T(8,128)S(1)}, f32[16,512]{1,0:T(8,128)S(1)}) custom-call(s32[1]{0:T(128)} %copy.22.step_ref, s32[4]{0:T(128)S(1)} %copy-done.4, bf16[1,4,16,512]{3,2,1,0:T(8,128)(2,1)S(1)} %copy.23.inner_ref, f32[4,16,512]{2,1,0:T(8,128)S(1)} %copy.24.outer_ref, bf16[256,4096]{1,0:T(8,128)(2,1)S(1)} %copy-done.2, bf16[256,512]{1,0:T(8,128)(2,1)S(1)} %copy-done.3), custom_call_target="tpu_custom_call" | custom-call | flops 1073741824 | bytes 2097152 | tf_op jit(solution)/shard_map/exchange/pallas_call | solution.py:209
  95.5 0.7 fusion.7
  96.2 0.0 copy-done.8
  96.2 0.0 copy-done.6
  96.2 0.0 copy-done.7
  96.2 0.0 copy-start.1
  96.2 1.2 %fusion.2 = (bf16[1,16,512]{2,1,0:T(8,128)(2,1)}, f32[1,16,512]{2,1,0:T(8,128)}, f32[1,16,512]{2,1,0:T(8,128)}, f32[4,16,512]{2,1,0:T(8,128)S(1)}, f32[4,16,512]{2,1,0:T(8,128)S(1)}) fusion(bf16[1,16,512]{2,1,0:T(8,128)(2,1)S(1)} %copy-done.8, f32[]{:T(128)S(6)} %sub.14, f32[]{:T(128)S(6)} %sub.13, f32[16,512]{1,0:T(8,128)S(1)} %get-tuple-element.46, ...), kind=kLoop, calls=%fused_computation.5 | loop fusion | flops 229376 | bytes 360462 | tf_op jit(solution)/shard_map/convert_element_type | solution.py:58
  97.4 0.0 copy-start
  97.4 0.0 copy-start.5
  97.4 0.0 copy-done.1
  97.5 0.6 copy-done
  98.1 0.0 copy-done.5
Async XLA Ops:
  2.4 93.7 %copy-start.8 = (bf16[1,16,512]{2,1,0:T(8,128)(2,1)S(1)}, bf16[1,16,512]{2,1,0:T(8,128)(2,1)}, u32[]{:S(2)}) copy-start(bf16[1,16,512]{2,1,0:T(8,128)(2,1)} %param.25) | copy-start | bytes 49156
  3.3 92.9 %copy-start.6 = (f32[1,16,512]{2,1,0:T(8,128)S(1)}, f32[1,16,512]{2,1,0:T(8,128)}, u32[]{:S(2)}) copy-start(f32[1,16,512]{2,1,0:T(8,128)} %param.27) | copy-start | bytes 98308
  3.3 92.9 %copy-start.7 = (f32[1,16,512]{2,1,0:T(8,128)S(1)}, f32[1,16,512]{2,1,0:T(8,128)}, u32[]{:S(2)}) copy-start(f32[1,16,512]{2,1,0:T(8,128)} %param.26) | copy-start | bytes 98308
  10.0 1.6 %copy-start.2 = (bf16[256,4096]{1,0:T(8,128)(2,1)S(1)}, bf16[256,4096]{1,0:T(8,128)(2,1)}, u32[]{:S(2)}) copy-start(bf16[256,4096]{1,0:T(8,128)(2,1)} %act_ref.1) | copy-start | bytes 6291460
  11.6 0.9 copy-start.3
  12.5 0.7 copy-start.4
  96.2 1.2 %copy-start.1 = (bf16[1,4,16,512]{3,2,1,0:T(8,128)(2,1)}, bf16[1,4,16,512]{3,2,1,0:T(8,128)(2,1)S(1)}, u32[]{:S(2)}) copy-start(bf16[1,4,16,512]{3,2,1,0:T(8,128)(2,1)S(1)} %fusion.7) | copy-start | bytes 196612
  97.4 0.7 copy-start
  97.4 0.7 copy-start.5

commit v2 on v1

v2 whole, which is shorter than its diff:
```python
import math

import jax
import jax.numpy as jnp
from jax import lax
from jax.experimental import pallas as pl
from jax.experimental.pallas import tpu as pltpu
from jax.sharding import PartitionSpec as P

BLOCK = 128
FRAGS = 4

BETA_FIRST = 0.9
BETA_SECOND = 0.95
INNER_RATE = 0.05
DECAY_RATE = 0.1
ADAM_EPSILON = 1e-08
OUTER_RATE = 0.7
OUTER_MOMENTUM = 0.9
CODE_LIMIT = 448.0
SCALE_EPSILON = 1e-06

ROWS = 16
COLS = 512
LANES = 4096
QUARTER = COLS // 4
PLANES = 8
WIDTH = 512
BLOCKS = WIDTH // ROWS
MESH = pl.DeviceIdType.MESH

CHUNKS = (3, 5, 4, 2, 6, 1, 7, 0)
QUARTERS = ("aby", "bay", "yab", "yba")
MOVES = (
    (("y", 2, 2), ("a", 0, 1), ("b", 1, 1)),
    (("b", 0, 1), ("a", 1, 2), ("b", 3, 1)),
    (("y", 0, 2), ("b", 2, 1), ("a", 3, 1)),
)
LAGS = (1, 2, 3, 4)


def exchange(
    step_hbm, ids_hbm, inner_hbm, outer_hbm, act_hbm, cot_hbm,
    grad_ref, sum_ref,
    step_ref, ids_ref, inner_ref, outer_ref, act_ref, cot_ref,
    work, got, last, terms,
    load, load_act, send, recv, term_send, term_recv, above, below,
):
    rep = lax.axis_index("replica")
    me = lax.axis_index("fsdp")
    x = lax.rem(me, 4)
    y = lax.rem(me // 4, 2)
    z = me // 8
    low = lax.rem(z, 4)
    high = z // 4
    a = lax.rem((x + 1) // 2, 2)
    b = x // 2

    def at(x_to, y_to, low_to, high_to):
        return (rep, ((high_to * 4 + low_to) * 2 + y_to) * 4 + x_to)

    along_a = at(x + 1 - 2 * lax.rem(x, 2), y, low, high)
    along_b = at(3 - x, y, low, high)
    along_y = at(x, 1 - y, low, high)
    lows = [at(x, y, lax.rem(low + i, 4), high) for i in range(1, 4)]
    highs = {d: at(x, y, low, lax.rem(high + d, PLANES)) for d in range(1, PLANES)}
    up, down = highs[1], highs[PLANES - 1]
    reps = [(lax.rem(rep + i, 4), me) for i in range(1, 4)]

    def signal(semaphore, peer):
        pl.semaphore_signal(semaphore, inc=1, device_id=peer, device_id_type=MESH)

    barrier = pltpu.get_barrier_semaphore()
    peers = [up, down, *lows, along_y, along_a, along_b, *reps]
    for peer in peers:
        signal(barrier, peer)

    count = len(CHUNKS)

    def columns(c):
        return pl.ds(pl.multiple_of(lax.rem(high + CHUNKS[c], PLANES) * WIDTH, WIDTH), WIDTH)

    def load_chunk(c):
        return pltpu.make_async_copy(
            act_hbm.at[:, columns(c)], act_ref.at[:, columns(c)], load_act.at[c]
        )

    loads = [
        pltpu.make_async_copy(src, dst, load.at[i])
        for i, (src, dst) in enumerate(
            (
                (cot_hbm, cot_ref),
                (step_hbm, step_ref),
                (ids_hbm, ids_ref),
                (inner_hbm, inner_ref),
                (outer_hbm, outer_ref),
            )
        )
    ]
    loads[0].start()
    for c in range(count):
        load_chunk(c).start()
    for copy in loads[1:]:
        copy.start()

    def remote(src, dst, sems, k, peer):
        return pltpu.make_async_remote_copy(
            src_ref=src, dst_ref=dst, send_sem=sems[0].at[k], recv_sem=sems[1].at[k],
            device_id=peer, device_id_type=MESH,
        )

    def multiply(c):
        load_chunk(c).wait()
        part = lax.dot_general(
            act_ref[:, columns(c)], cot_ref[...], (((0,), (0,)), ((), ())),
            preferred_element_type=jnp.float32,
        ).astype(jnp.bfloat16)
        for n in range(BLOCKS):
            low_to, y_to, x_to = n // 8, (n // 4) % 2, n % 4
            off_a = lax.rem(a + ((x_to + 1) // 2) % 2, 2)
            off_b = lax.rem(b + x_to // 2, 2)
            off_y = lax.rem(y + y_to, 2)
            off_m = lax.rem(low_to - low + 4, 4)
            off = {"a": off_a, "b": off_b, "y": off_y}
            for q, order in enumerate(QUARTERS):
                place = off_m
                for stage, axis in enumerate(order):
                    place = place + off[axis] * (16 >> stage)
                work[c, q, place] = part[
                    n * ROWS : (n + 1) * ROWS, q * QUARTER : (q + 1) * QUARTER
                ]

    along = {"a": along_a, "b": along_b, "y": along_y}

    def sends(c, stage):
        sems = (send.at[c], recv.at[c])
        if stage == 4:
            ahead = CHUNKS[c]
            if not ahead:
                return []
            return [remote(work.at[c, :, 0], last.at[ahead - 1], sems, 12, highs[ahead])]
        if stage == 3:
            return [
                remote(work.at[c, :, i], got.at[c, :, 27 + i], sems, 8 + i, lows[i - 1])
                for i in range(1, 4)
            ]
        held, landed = 16 >> stage, 32 - (32 >> stage)
        return [
            remote(
                work.at[c, pl.ds(q, n), pl.ds(held, held)], got.at[c, pl.ds(q, n), pl.ds(landed, held)],
                sems, 3 * stage + i, along[axis],
            )
            for i, (axis, q, n) in enumerate(MOVES[stage])
        ]

    def advance(c, stage):
        for copy in sends(c, stage):
            copy.wait_recv()
        if stage == 3:
            for q in range(4):
                total = work[c, q, 0].astype(jnp.float32)
                for i in range(28, 31):
                    total = total + got[c, q, i].astype(jnp.float32)
                if CHUNKS[c]:
                    work[c, q, 0] = total.astype(jnp.bfloat16)
                else:
                    grad_ref[:, q * QUARTER : (q + 1) * QUARTER] = total
        else:
            held, landed = 16 >> stage, 32 - (32 >> stage)

            def some(i, carry):
                mine, theirs = pl.ds(i * 4, 4), pl.ds(landed + i * 4, 4)
                for q in range(4):
                    total = work[c, q, mine].astype(jnp.float32)
                    total = total + got[c, q, theirs].astype(jnp.float32)
                    work[c, q, mine] = total.astype(jnp.bfloat16)
                return carry

            lax.fori_loop(0, held // 4, some, 0)
        for copy in sends(c, stage + 1):
            copy.start()

    loads[0].wait()
    multiply(0)
    pl.semaphore_wait(barrier, len(peers))
    signal(above.at[0], down)
    signal(below.at[0], up)
    swaps = [
        remote(terms.at[rep], terms.at[rep], (term_send, term_recv), i, reps[i]) for i in range(3)
    ]
    for t in range(count + LAGS[-1]):
        if t < count:
            if t:
                multiply(t)
            for copy in sends(t, 0):
                copy.start()
        if t == 0:
            for copy in loads[1:]:
                copy.wait()
            frag = ids_ref[lax.rem(step_ref[0], FRAGS)]
            deltas = outer_ref[frag] - inner_ref[0, frag].astype(jnp.float32)
            for k in range(COLS // BLOCK):
                part = deltas[:, k * BLOCK : (k + 1) * BLOCK]
                scale = (
                    jnp.max(jnp.abs(part), axis=-1, keepdims=True) / CODE_LIMIT + SCALE_EPSILON
                )
                coded = (part / scale).astype(jnp.bfloat16).astype(jnp.float32)
                terms[rep, :, k * BLOCK : (k + 1) * BLOCK] = (coded * scale).astype(jnp.bfloat16)
            for copy in swaps:
                copy.start()
        if 1 <= t <= 3:
            pl.semaphore_wait(above.at[t - 1], 1)
            if t < 3:
                pl.semaphore_wait(below.at[t - 1], 1)
                signal(above.at[t], down)
            if t < 2:
                signal(below.at[t], up)
        if t == count - 1:
            for copy in swaps:
                copy.wait()
            total = terms[0].astype(jnp.float32)
            for i in range(1, 4):
                total = total + terms[i].astype(jnp.float32)
            sum_ref[...] = total
        for stage, lag in enumerate(LAGS):
            if 0 <= t - lag < count:
                advance(t - lag, stage)

    for c in range(count):
        for copy in sends(c, 4):
            copy.wait_recv()
    for q in range(4):
        lanes = slice(q * QUARTER, (q + 1) * QUARTER)
        total = grad_ref[:, lanes]
        for i in range(PLANES - 1):
            total = total + last[i, q].astype(jnp.float32)
        grad_ref[:, lanes] = total
    for c in range(count):
        for stage in range(5):
            for copy in sends(c, stage):
                copy.wait_send()


def exchanged(step_count, layer_ids, inner_stack, outer_stack, activations, cotangent):
    vmem = pl.BlockSpec(memory_space=pltpu.VMEM)
    hbm = pl.BlockSpec(memory_space=pltpu.HBM)
    n = len(CHUNKS)
    block = (ROWS, QUARTER)
    tokens, features = activations.shape
    return pl.pallas_call(
        exchange,
        name="exchange",
        out_shape=(jax.ShapeDtypeStruct((ROWS, COLS), jnp.float32),) * 2,
        in_specs=[hbm] * 6,
        out_specs=(vmem, vmem),
        scratch_shapes=[
            pltpu.SMEM(step_count.shape, jnp.int32),
            pltpu.SMEM(layer_ids.shape, jnp.int32),
            pltpu.VMEM(inner_stack.shape, jnp.bfloat16),
            pltpu.VMEM(outer_stack.shape, jnp.float32),
            pltpu.VMEM(activations.shape, jnp.bfloat16),
            pltpu.VMEM(cotangent.shape, jnp.bfloat16),
            pltpu.VMEM((n, 4, BLOCKS) + block, jnp.bfloat16),
            pltpu.VMEM((n, 4, BLOCKS - 1) + block, jnp.bfloat16),
            pltpu.VMEM((PLANES - 1, 4) + block, jnp.bfloat16),
            pltpu.VMEM((4, ROWS, COLS), jnp.bfloat16),
            pltpu.SemaphoreType.DMA((5,)),
            pltpu.SemaphoreType.DMA((n,)),
            pltpu.SemaphoreType.DMA((n, 13)),
            pltpu.SemaphoreType.DMA((n, 13)),
            pltpu.SemaphoreType.DMA((3,)),
            pltpu.SemaphoreType.DMA((3,)),
            pltpu.SemaphoreType.REGULAR((3,)),
            pltpu.SemaphoreType.REGULAR((2,)),
        ],
        compiler_params=pltpu.CompilerParams(
            collective_id=0, has_side_effects=True, vmem_limit_bytes=62 * 2**20
        ),
        cost_estimate=pl.CostEstimate(
            flops=2 * tokens * features * COLS, bytes_accessed=2 * tokens * features, transcendentals=0
        ),
    )(step_count, layer_ids, inner_stack, outer_stack, activations, cotangent)


def finish(
    step_ref, ids_ref, sum_ref, grad_ref, inner_ref, outer_ref, moment_ref, key_ref, first_ref, second_ref,
    inner_out, outer_out, moment_out, key_out, first_out, second_out,
):
    frag = ids_ref[lax.rem(step_ref[0], FRAGS)]
    average = sum_ref[...] / 4
    outer_frag = outer_ref[frag]
    moment_new = OUTER_MOMENTUM * moment_ref[frag] + average
    outer_new = outer_frag - OUTER_RATE * (OUTER_MOMENTUM * moment_new + average)
    rounded = outer_new.astype(jnp.bfloat16)
    for layer in range(outer_ref.shape[0]):
        taken = frag == layer
        inner_out[0, layer] = jnp.where(taken, rounded, inner_ref[0, layer])
        outer_out[layer] = jnp.where(taken, outer_new, outer_ref[layer])
        moment_out[layer] = jnp.where(taken, moment_new, moment_ref[layer])

    gradient = grad_ref[...]
    counter = jnp.full((8, 128), step_ref[0] + 1, jnp.int32).astype(jnp.float32)
    first_left = 1.0 - jnp.exp(counter * math.log(BETA_FIRST))[:1, :1]
    second_left = 1.0 - jnp.exp(counter * math.log(BETA_SECOND))[:1, :1]
    first_new = BETA_FIRST * first_ref[0] + (1.0 - BETA_FIRST) * gradient
    second_new = BETA_SECOND * second_ref[0] + (1.0 - BETA_SECOND) * gradient * gradient
    first_hat = first_new / first_left
    second_hat = second_new / second_left
    widened = key_ref[0].astype(jnp.float32)
    moved = widened - INNER_RATE * (
        first_hat / (jnp.sqrt(second_hat) + ADAM_EPSILON) + DECAY_RATE * widened
    )
    key_out[0] = moved.astype(jnp.bfloat16)
    first_out[0] = first_new
    second_out[0] = second_new


def on_device(
    inner_stack,
    outer_stack,
    outer_moment,
    layer_ids,
    step_count,
    activations,
    cotangent,
    key_weight,
    first_moment,
    second_moment,
):
    gradient, summed = exchanged(
        step_count, layer_ids, inner_stack, outer_stack, activations, cotangent
    )
    vmem = pl.BlockSpec(memory_space=pltpu.VMEM)
    smem = pl.BlockSpec(memory_space=pltpu.SMEM)
    like = (inner_stack, outer_stack, outer_moment, key_weight, first_moment, second_moment)
    return pl.pallas_call(
        finish,
        name="finish",
        out_shape=tuple(jax.ShapeDtypeStruct(v.shape, v.dtype) for v in like),
        in_specs=[smem] * 2 + [vmem] * 8,
        out_specs=(vmem,) * 6,
    )(step_count, layer_ids, summed, gradient, *like)


def solution(mesh):
    return jax.shard_map(
        on_device,
        mesh=mesh,
        in_specs=(
            P("replica", None, "fsdp", None),
            P(None, "fsdp", None),
            P(None, "fsdp", None),
            P(),
            P(),
            P(("replica", "fsdp"), None),
            P(("replica", "fsdp"), None),
            P("replica", "fsdp", None),
            P("replica", "fsdp", None),
            P("replica", "fsdp", None),
        ),
        out_specs=(
            P("replica", None, "fsdp", None),
            P(None, "fsdp", None),
            P(None, "fsdp", None),
            P("replica", "fsdp", None),
            P("replica", "fsdp", None),
            P("replica", "fsdp", None),
        ),
        check_vma=False,
    )
```

time: 98.6 us -> 70.2 us (0.71)
  the two profiles are of different devices: /device:TPU:2 before, /device:TPU:6 now
where the time goes in v2:
time: 70.2 us; the launch traced here: 69.3 us
  Pallas kernels  68 us (97%)
  between operations  1.29 us (2%)
    pallas_call x1, Pallas kernels, exchanged(): pl.pallas_call(exchange, name='exchange', out_shape=(jax.ShapeDtypeStruct...  66.2 us
    pallas_call x1, Pallas kernels, on_device(): pl.pallas_call(finish, name='finish', out_shape=tuple((jax.ShapeDtypeStru...  1.84 us

profile of v2, /device:TPU:6, one launch (start us, length us, event | category | flops | bytes accessed | tf_op | source)
XLA Modules:
  0.0 69.3 jit_solution(12088451152023631126)
XLA Ops:
  1.3 66.2 %exchange.1 = (f32[16,512]{1,0:T(8,128)}, f32[16,512]{1,0:T(8,128)}) custom-call(s32[1]{0:T(128)S(6)} %copy.16.step_hbm.step_ref, s32[4]{0:T(128)} %ids_ref.1, bf16[1,4,16,512]{3,2,1,0:T(8,128)(2,1)} %inner_ref.1, f32[4,16,512]{2,1,0:T(8,128)} %outer_ref.1, bf16[256,4096]{1,0:T(8,128)(2,1)} %act_hbm.1, bf16[256,512]{1,0:T(8,128)(2,1)} %cot_hbm.1), custom_call_target="tpu_custom_call" | custom-call | flops 1073741824 | bytes 2097152 | tf_op jit(solution)/shard_map/exchange/pallas_call | solution.py:250
  67.4 1.8 %finish.1 = (bf16[1,4,16,512]{3,2,1,0:T(8,128)(2,1)}, f32[4,16,512]{2,1,0:T(8,128)}, f32[4,16,512]{2,1,0:T(8,128)}, bf16[1,16,512]{2,1,0:T(8,128)(2,1)}, f32[1,16,512]{2,1,0:T(8,128)}, /*index=5*/f32[1,16,512]{2,1,0:T(8,128)}) custom-call(s32[1]{0:T(128)S(6)} %copy.16.step_hbm.step_ref, s32[4]{0:T(128)} %ids_ref.1, f32[16,512]{1,0:T(8,128)} %get-tuple-element.8.sum_ref, ...), custom_call_target="tpu_custom_call" | custom-call | tf_op jit(solution)/shard_map/finish/pallas_call | solution.py:336

commit v3 on v2

--- a/solution.py
+++ b/solution.py
@@ -190,11 +190,11 @@
     ]
     for t in range(count + LAGS[-1]):
         if t < count:
-            if t:
-                multiply(t)
             for copy in sends(t, 0):
                 copy.start()
-        if t == 0:
+        if t + 1 < count:
+            multiply(t + 1)
+        if t == 2:
             for copy in loads[1:]:
                 copy.wait()
             frag = ids_ref[lax.rem(step_ref[0], FRAGS)]

time: 70.2 us -> 69.8 us (level)
  no operation moved by 1% of the time
where the time goes in v3:
time: 69.8 us; the launch traced here: 69.6 us
  Pallas kernels  68.3 us (98%)
  between operations  1.29 us (2%)
    pallas_call x1, Pallas kernels, exchanged(): pl.pallas_call(exchange, name='exchange', out_shape=(jax.ShapeDtypeStruct...  66.4 us
    pallas_call x1, Pallas kernels, on_device(): pl.pallas_call(finish, name='finish', out_shape=tuple((jax.ShapeDtypeStru...  1.84 us

profile of v3, /device:TPU:6, one launch (start us, length us, event | category | flops | bytes accessed | tf_op | source)
XLA Modules:
  0.0 69.6 jit_solution(3856530858479365623)
XLA Ops:
  1.3 66.4 %exchange.1 = (f32[16,512]{1,0:T(8,128)}, f32[16,512]{1,0:T(8,128)}) custom-call(s32[1]{0:T(128)S(6)} %copy.16.step_hbm.step_ref, s32[4]{0:T(128)} %ids_ref.1, bf16[1,4,16,512]{3,2,1,0:T(8,128)(2,1)} %inner_ref.1, f32[4,16,512]{2,1,0:T(8,128)} %outer_ref.1, bf16[256,4096]{1,0:T(8,128)(2,1)} %act_hbm.1, bf16[256,512]{1,0:T(8,128)(2,1)} %cot_hbm.1), custom_call_target="tpu_custom_call" | custom-call | flops 1073741824 | bytes 2097152 | tf_op jit(solution)/shard_map/exchange/pallas_call | solution.py:250
  67.7 1.8 %finish.1 = (bf16[1,4,16,512]{3,2,1,0:T(8,128)(2,1)}, f32[4,16,512]{2,1,0:T(8,128)}, f32[4,16,512]{2,1,0:T(8,128)}, bf16[1,16,512]{2,1,0:T(8,128)(2,1)}, f32[1,16,512]{2,1,0:T(8,128)}, /*index=5*/f32[1,16,512]{2,1,0:T(8,128)}) custom-call(s32[1]{0:T(128)S(6)} %copy.16.step_hbm.step_ref, s32[4]{0:T(128)} %ids_ref.1, f32[16,512]{1,0:T(8,128)} %get-tuple-element.8.sum_ref, ...), custom_call_target="tpu_custom_call" | custom-call | tf_op jit(solution)/shard_map/finish/pallas_call | solution.py:336
